TPU v7x, 32 devices: a whole 2x2x4 slice. The times are simulated.
32 devices in a mesh: rec: 2 (over y), leaf: 4 (over z), rhs: 2 (over x), pan: 2 (over core).
Axes of the slice: x: 2, y: 2, z: 4, core: 2. Of those that a mesh axis runs over, the one named last changes fastest.
Arguments:
- bottom_source: bfloat16 [32768, 256], P(('rec', 'leaf', 'rhs', 'pan')), parts along dimension 0, may hold values from -6 to 6
- bottom_inverse: bfloat16 [32768, 1024], P(('rec', 'leaf', 'rhs', 'pan')), parts along dimension 0, as said below
- bottom_update: bfloat16 [4096, 1024], P(('rec', 'leaf', 'rhs', 'pan')), parts along dimension 0, may hold values from -0.0625 to 0.0625
- bottom_sensitivity: bfloat16 [1024, 16384], P('rec', ('leaf', 'rhs', 'pan')), parts along dimension 0, may hold values from -0.03125 to 0.03125
- bottom_order: int32 [16, 1024], P(('leaf', 'rhs', 'pan')), may hold values from 0 to 1023, each once within a row
- bottom_extent: int32 [16], P(('leaf', 'rhs', 'pan')), may hold values from 384 to 1024, as said below
- bottom_targets: int32 [16, 128], P(('leaf', 'rhs', 'pan')), may hold values from 0 to 255, as said below
- upper_source: bfloat16 [3584, 256], P(('rec', 'leaf'), ('rhs', 'pan')), parts along dimension 0, may hold values from -6 to 6
- upper_inverse: bfloat16 [3584, 256], P(('rec', 'leaf')), parts along dimension 0, as said below
- upper_update: bfloat16 [256, 1536], P('rec', 'leaf'), parts along dimension 0, may hold values from -0.25 to 0.25
- upper_targets: int32 [6, 128], replicated, may hold values from 0 to 255, as said below
Outputs:
- adjoint: bfloat16 [32768, 256], P(('rec', 'leaf', 'rhs', 'pan')), parts along dimension 0
- gradient: float32 [1024, 256], P(('rec', 'leaf', 'rhs', 'pan')), parts along dimension 0
There are 2 independent parts, one for each index of `rec`. A program takes and returns all parts, laid end to end along the dimension named above; an argument that names none is the same for every part. Nothing has to cross between parts.
Inputs may be any that keep to these rules, and one draw needn't show every extreme that they name: `bottom_inverse`: lower triangular, with its diagonal between 0.6 and 1.4. `upper_inverse`: lower triangular in each front's row order, with its diagonal between 0.6 and 1.4. `bottom_extent`: a multiple of 128; some front uses all 1024 rows. `bottom_targets`: the rows of one front go to distinct rows. `upper_targets`: the rows of one front go to distinct rows.
All inputs are finite; a program needn't handle non-finite values.
Results may differ from a plain program's by a relative error of at most 0.0058.
Values may be sent and summed in bfloat16 or wider, within the bound.
A program may use at most 64 MiB of HBM per device.

v0:
```python
import jax
import jax.numpy as jnp
from jax import lax
from jax.sharding import PartitionSpec as P


def partner(value, axis, apart):
    mask = 2**apart
    pairs = [(source, source ^ mask) for source in range(lax.axis_size(axis))]
    return lax.ppermute(value, axis, pairs)


def climb_sum(values, bit_count):
    for bit_index in range(bit_count):
        values = values + partner(values, "leaf", bit_index)
    return values


def descend_sum(values, bit_count):
    for bit_index in range(bit_count):
        values = values + partner(values, "leaf", bit_index)
    return values


def shards(
    bottom_source,
    bottom_inverse,
    bottom_update,
    bottom_sensitivity,
    bottom_order,
    bottom_extent,
    bottom_targets,
    upper_source,
    upper_inverse,
    upper_update,
    upper_targets,
):
    leaves = lax.axis_size("leaf")
    depth = leaves.bit_length() - 1
    leaf_place = lax.axis_index("leaf")
    front_rows = bottom_inverse.shape[0]
    front_size = upper_inverse.shape[1]
    order_rows = bottom_order[0]
    row_mask = (jnp.arange(front_rows, dtype=jnp.int32) < bottom_extent[0]).astype(jnp.bfloat16)[
        :, None
    ]
    ordered = bottom_source[order_rows] * row_mask
    solved = (
        jnp.dot(bottom_inverse, ordered, preferred_element_type=jnp.float32) * row_mask
    ).astype(jnp.bfloat16)
    contrib = jnp.dot(bottom_update, solved, preferred_element_type=jnp.float32)
    spread = (
        jnp.zeros((front_size, contrib.shape[1]), jnp.float32).at[bottom_targets[0]].set(contrib)
    )
    summed = lax.psum(spread, ("rhs", "pan"))
    loads = lax.all_gather(upper_source, ("rhs", "pan"), axis=1, tiled=True)
    column_count = summed.shape[1]
    front_input = (loads[0:front_size].astype(jnp.float32) - summed).astype(jnp.bfloat16)
    solved_upper = []
    for height in range(depth + 1):
        row_count = front_size >> height
        offset = 2 * front_size - (2 * front_size >> height)
        inverse_now = upper_inverse[offset : offset + row_count]
        solved_front = jnp.dot(inverse_now, front_input, preferred_element_type=jnp.float32).astype(
            jnp.bfloat16
        )
        solved_upper.append(solved_front)
        if height < depth:
            update_now = upper_update[:, offset : offset + row_count]
            lifted = jnp.dot(update_now, solved_front, preferred_element_type=jnp.float32)
            map_row = 2 * leaves - (2 * leaves >> height) + leaf_place // (1 << height)
            targets = lax.dynamic_slice_in_dim(upper_targets, map_row, 1, 0)[0]
            partial_input = (
                jnp.zeros((front_size, column_count), jnp.float32).at[targets].set(-lifted)
            )
            parent_rows = front_size >> height + 1
            parent_offset = 2 * front_size - (2 * front_size >> height + 1)
            parent_place = leaf_place % (2 << height) * parent_rows
            own_load = loads[parent_offset : parent_offset + parent_rows].astype(jnp.float32)
            current = lax.dynamic_slice_in_dim(partial_input, parent_place, parent_rows, 0)
            partial_input = lax.dynamic_update_slice_in_dim(
                partial_input, current + own_load, parent_place, 0
            )
            front_input = climb_sum(partial_input, height + 1).astype(jnp.bfloat16)
    back_rows = None
    for height in range(depth, -1, -1):
        row_count = front_size >> height
        offset = 2 * front_size - (2 * front_size >> height)
        inverse_now = upper_inverse[offset : offset + row_count]
        if height == depth:
            residue = solved_upper[height]
        else:
            map_row = 2 * leaves - (2 * leaves >> height) + leaf_place // (1 << height)
            targets = lax.dynamic_slice_in_dim(upper_targets, map_row, 1, 0)[0]
            picked = back_rows[targets]
            update_now = upper_update[:, offset : offset + row_count]
            coupled = jnp.einsum(
                "rj,rc->jc", update_now, picked, preferred_element_type=jnp.float32
            )
            residue = (solved_upper[height].astype(jnp.float32) - coupled).astype(jnp.bfloat16)
        partial_back = jnp.einsum(
            "ij,ic->jc", inverse_now, residue, preferred_element_type=jnp.float32
        )
        back_rows = descend_sum(partial_back, height).astype(jnp.bfloat16)
    picked_root = back_rows[bottom_targets[0]]
    coupled_root = jnp.einsum(
        "rj,rc->jc", bottom_update, picked_root, preferred_element_type=jnp.float32
    )
    bottom_residue = ((solved.astype(jnp.float32) - coupled_root) * row_mask).astype(jnp.bfloat16)
    bottom_back = (
        jnp.einsum("ij,ic->jc", bottom_inverse, bottom_residue, preferred_element_type=jnp.float32)
        * row_mask
    ).astype(jnp.bfloat16)
    adjoint = jnp.zeros_like(bottom_back).at[order_rows].set(bottom_back)
    gradient = lax.psum_scatter(
        -jnp.dot(bottom_sensitivity, adjoint, preferred_element_type=jnp.float32),
        ("leaf", "rhs", "pan"),
        scatter_dimension=0,
        tiled=True,
    )
    return (adjoint, gradient)


def solution(mesh):
    placed = (
        P(("rec", "leaf", "rhs", "pan"), None),
        P(("rec", "leaf", "rhs", "pan"), None),
        P(("rec", "leaf", "rhs", "pan"), None),
        P("rec", ("leaf", "rhs", "pan")),
        P(("leaf", "rhs", "pan"), None),
        P(("leaf", "rhs", "pan")),
        P(("leaf", "rhs", "pan"), None),
        P(("rec", "leaf"), ("rhs", "pan")),
        P(("rec", "leaf"), None),
        P("rec", "leaf"),
        P(),
    )
    return jax.shard_map(
        shards,
        mesh=mesh,
        in_specs=placed,
        out_specs=(P(("rec", "leaf", "rhs", "pan"), None), P(("rec", "leaf", "rhs", "pan"), None)),
        check_vma=False,
    )
```

profile of v0, /device:TPU:0, one launch (start us, length us, event | category | flops | bytes accessed | tf_op | source)
XLA Modules:
  0.0 189.3 jit_solution(15696807839329698646)
XLA Ops:
  9.4 4.6 %gather_fusion = bf16[1024,256]{1,0:T(8,128)(2,1)S(1)} fusion(bf16[1024,256]{1,0:T(8,128)(2,1)} %param.11, s32[1024]{0:T(1024)S(1)} %broadcast_clamp_fusion), kind=kCustom, calls=%fused_computation | custom fusion | bytes 1052672 | tf_op jit(solution)/shard_map/gather | solution.py:47
  14.0 1.0 fusion.3
  15.0 0.8 copy-done.3
  16.2 1.7 scatter_custom_fusion
  18.0 7.2 %all_gather.3 = bf16[448,256]{0,1:T(8,128)(2,1)S(1)} all-gather(bf16[448,64]{0,1:T(8,128)(2,1)S(1)} %copy-done.7), channel_id=1, replica_groups=mesh['rec'=2,'leaf'=4,'rhs'=2,'pan'=2] {'rhs','pan'}, dimensions={1}, use_global_device_ids=true | all-gather | bytes 286720 | tf_op jit(solution)/shard_map/all_gather | solution.py:56
  25.5 0.8 fusion.45
  26.3 26.5 %all-reduce.2.cloned.1.call-done = f32[256,256]{1,0:T(8,128)} async-done(((f32[256,256]{1,0:T(8,128)}), f32[256,256]{1,0:T(8,128)}) %all-reduce.2.cloned.1.call-update) | async-done | bytes 262160 | tf_op jit(solution)/shard_map/psum | solution.py:55
  52.8 1.2 convolution_convert_fusion.1
  54.2 1.1 scatter_custom_fusion.1
  55.4 1.6 collective-permute-start
  57.0 5.1 %collective-permute-done = f32[256,256]{1,0:T(8,128)S(1)} collective-permute-done((f32[256,256]{1,0:T(8,128)S(1)}, f32[256,256]{1,0:T(8,128)S(1)}, u32[]{:S(2)}, u32[]{:S(2)}) %collective-permute-start) | collective-permute-done | bytes 262176 | tf_op jit(solution)/shard_map/ppermute | solution.py:10
  62.6 1.1 scatter_custom_fusion.2
  63.7 1.8 collective-permute-start.1
  65.5 4.6 %collective-permute-done.1 = f32[256,256]{1,0:T(8,128)S(1)} collective-permute-done((f32[256,256]{1,0:T(8,128)S(1)}, f32[256,256]{1,0:T(8,128)S(1)}, u32[]{:S(2)}, u32[]{:S(2)}) %collective-permute-start.1) | collective-permute-done | bytes 262176 | tf_op jit(solution)/shard_map/ppermute | solution.py:10
  70.2 3.3 %collective-permute-start.2 = (f32[256,256]{1,0:T(8,128)S(1)}, f32[256,256]{1,0:T(8,128)S(1)}, u32[]{:S(2)}, u32[]{:S(2)}) collective-permute-start(f32[256,256]{1,0:T(8,128)S(1)} %add.117), channel_id=1, source_target_pairs={{0,8},{4,12},{8,0},{12,4},{1,9},{5,13},{9,1},{13,5},{2,10},{6,14},... | collective-permute-start | bytes 786440 | tf_op jit(solution)/shard_map/ppermute | solution.py:10
  73.5 8.1 %collective-permute-done.2 = f32[256,256]{1,0:T(8,128)S(1)} collective-permute-done((f32[256,256]{1,0:T(8,128)S(1)}, f32[256,256]{1,0:T(8,128)S(1)}, u32[]{:S(2)}, u32[]{:S(2)}) %collective-permute-start.2) | collective-permute-done | bytes 262176 | tf_op jit(solution)/shard_map/ppermute | solution.py:10
  82.0 0.8 collective-permute-start.3
  82.8 5.6 %collective-permute-done.3 = f32[256,256]{0,1:T(8,128)S(1)} collective-permute-done((f32[256,256]{0,1:T(8,128)S(1)}, f32[256,256]{0,1:T(8,128)S(1)}, u32[]{:S(2)}, u32[]{:S(2)}) %collective-permute-start.3) | collective-permute-done | bytes 262176 | tf_op jit(solution)/shard_map/ppermute | solution.py:10
  88.5 2.8 %collective-permute-start.4 = (f32[256,256]{0,1:T(8,128)S(1)}, f32[256,256]{0,1:T(8,128)S(1)}, u32[]{:S(2)}, u32[]{:S(2)}) collective-permute-start(f32[256,256]{0,1:T(8,128)S(1)} %add.119), channel_id=1, source_target_pairs={{0,8},{4,12},{8,0},{12,4},{1,9},{5,13},{9,1},{13,5},{2,10},{6,14},... | collective-permute-start | bytes 786440 | tf_op jit(solution)/shard_map/ppermute | solution.py:10
  91.3 9.9 %collective-permute-done.4 = f32[256,256]{0,1:T(8,128)S(1)} collective-permute-done((f32[256,256]{0,1:T(8,128)S(1)}, f32[256,256]{0,1:T(8,128)S(1)}, u32[]{:S(2)}, u32[]{:S(2)}) %collective-permute-start.4) | collective-permute-done | bytes 262176 | tf_op jit(solution)/shard_map/ppermute | solution.py:10
  101.3 0.8 gather_fusion.1
  102.2 1.1 convolution_bitcast_fusion
  103.3 0.8 collective-permute-start.5
  104.1 6.5 %collective-permute-done.5 = f32[256,256]{0,1:T(8,128)S(1)} collective-permute-done((f32[256,256]{0,1:T(8,128)S(1)}, f32[256,256]{0,1:T(8,128)S(1)}, u32[]{:S(2)}, u32[]{:S(2)}) %collective-permute-start.5) | collective-permute-done | bytes 262176 | tf_op jit(solution)/shard_map/ppermute | solution.py:10
  110.8 0.8 gather_fusion.2
  111.6 1.2 fusion.7
  112.9 0.8 gather_fusion.3
  113.8 1.8 fusion.4
  115.8 5.1 %scatter_custom_fusion.3 = bf16[1024,256]{1,0:T(8,128)(2,1)S(1)} fusion(s32[1024]{0:T(1024)S(1)} %bitcast.59, bf16[1024,256]{1,0:T(8,128)(2,1)S(1)} %copy.36, bf16[]{:T(256)} %constant.56.clone.1), kind=kCustom, calls=%fused_computation.42 | custom fusion | bytes 524290 | tf_op jit(solution)/shard_map/scatter | solution.py:114
  120.9 1.9 %fusion.5 = f32[512,256]{0,1:T(8,128)S(1)} fusion(bf16[1024,256]{1,0:T(8,128)(2,1)S(1)} %scatter_custom_fusion.3, bf16[512,1024]{1,0:T(8,128)(2,1)} %param.14), kind=kOutput, calls=%fused_computation.17 | convolution fusion | flops 268566528 | bytes 2097152 | tf_op jit(solution)/shard_map/dot_general | solution.py:116
  122.8 1.0 copy.38
  123.9 58.6 %reduce-scatter.4.cloned.1.call-done = f32[32,256]{1,0:T(8,128)} async-done(((f32[512,256]{1,0:T(8,128)}), f32[32,256]{1,0:T(8,128)}) %reduce-scatter.4.cloned.1.call-update) | async-done | bytes 32784
  (50 shorter events, 4.1 us)
Async XLA Ops:
  7.2 6.8 %copy-start = (bf16[1024,1024]{1,0:T(8,128)(2,1)S(1)}, bf16[1024,1024]{1,0:T(8,128)(2,1)}, u32[]{:S(2)}) copy-start(bf16[1024,1024]{1,0:T(8,128)(2,1)} %param.12) | copy-start | bytes 6291460
  7.2 45.6 %all-reduce.2.cloned.1.call-start = ((), (), s32[]{:S(2)}) async-start(), calls=%async_computation.1 | async-start | bytes 524288 | tf_op jit(solution)/shard_map/psum | solution.py:55
  14.0 1.8 copy-start.6
  14.0 4.0 %copy-start.7 = (bf16[448,64]{0,1:T(8,128)(2,1)S(1)}, bf16[448,64]{0,1:T(8,128)(2,1)}, u32[]{:S(2)}) copy-start(bf16[448,64]{0,1:T(8,128)(2,1)} %param.18) | copy-start | bytes 172036
  15.0 0.8 copy-start.3
  15.8 36.9 %copy-start.2 = (bf16[448,256]{1,0:T(8,128)(2,1)S(1)}, bf16[448,256]{1,0:T(8,128)(2,1)}, u32[]{:S(2)}) copy-start(bf16[448,256]{1,0:T(8,128)(2,1)} %param.19) | copy-start | bytes 688132
  15.8 38.1 %copy-start.5 = (bf16[128,384]{1,0:T(8,128)(2,1)S(1)}, bf16[128,384]{1,0:T(8,128)(2,1)}, u32[]{:S(2)}) copy-start(bf16[128,384]{1,0:T(8,128)(2,1)} %param.20) | copy-start | bytes 294916
  17.9 164.5 %reduce-scatter.4.cloned.1.call-start = ((), (), s32[]{:S(2)}) async-start(), calls=%async_computation.2 | async-start | bytes 557056
  55.4 6.7 %collective-permute-start = (f32[256,256]{1,0:T(8,128)S(1)}, f32[256,256]{1,0:T(8,128)S(1)}, u32[]{:S(2)}, u32[]{:S(2)}) collective-permute-start(f32[256,256]{1,0:T(8,128)S(1)} %add_dynamic-update-slice_fusion), channel_id=1, source_target_pairs={{0,4},{4,0},{8,12},{12,8},{1,5},{5,1},{9,13},{13,9},{2,6},{6,2},{1... | collective-permute-start | bytes 786440 | tf_op jit(solution)/shard_map/ppermute | solution.py:10
  63.7 6.4 %collective-permute-start.1 = (f32[256,256]{1,0:T(8,128)S(1)}, f32[256,256]{1,0:T(8,128)S(1)}, u32[]{:S(2)}, u32[]{:S(2)}) collective-permute-start(f32[256,256]{1,0:T(8,128)S(1)} %add_dynamic-update-slice_fusion.1), channel_id=1, source_target_pairs={{0,4},{4,0},{8,12},{12,8},{1,5},{5,1},{9,13},{13,9},{2,6},{6,2},{1... | collective-permute-start | bytes 786440 | tf_op jit(solution)/shard_map/ppermute | solution.py:10
  70.2 11.4 %collective-permute-start.2 = (f32[256,256]{1,0:T(8,128)S(1)}, f32[256,256]{1,0:T(8,128)S(1)}, u32[]{:S(2)}, u32[]{:S(2)}) collective-permute-start(f32[256,256]{1,0:T(8,128)S(1)} %add.117), channel_id=1, source_target_pairs={{0,8},{4,12},{8,0},{12,4},{1,9},{5,13},{9,1},{13,5},{2,10},{6,14},... | collective-permute-start | bytes 786440 | tf_op jit(solution)/shard_map/ppermute | solution.py:10
  82.0 6.4 %collective-permute-start.3 = (f32[256,256]{0,1:T(8,128)S(1)}, f32[256,256]{0,1:T(8,128)S(1)}, u32[]{:S(2)}, u32[]{:S(2)}) collective-permute-start(f32[256,256]{0,1:T(8,128)S(1)} %convolution_bitcast_fusion.1), channel_id=1, source_target_pairs={{0,4},{4,0},{8,12},{12,8},{1,5},{5,1},{9,13},{13,9},{2,6},{6,2},{1... | collective-permute-start | bytes 786440 | tf_op jit(solution)/shard_map/ppermute | solution.py:10
  88.5 12.7 %collective-permute-start.4 = (f32[256,256]{0,1:T(8,128)S(1)}, f32[256,256]{0,1:T(8,128)S(1)}, u32[]{:S(2)}, u32[]{:S(2)}) collective-permute-start(f32[256,256]{0,1:T(8,128)S(1)} %add.119), channel_id=1, source_target_pairs={{0,8},{4,12},{8,0},{12,4},{1,9},{5,13},{9,1},{13,5},{2,10},{6,14},... | collective-permute-start | bytes 786440 | tf_op jit(solution)/shard_map/ppermute | solution.py:10
  101.2 12.6 %copy-start.4 = (bf16[256,1024]{1,0:T(8,128)(2,1)S(1)}, bf16[256,1024]{1,0:T(8,128)(2,1)}, u32[]{:S(2)}) copy-start(bf16[256,1024]{1,0:T(8,128)(2,1)} %copy-done.3) | copy-start | bytes 1572868
  103.3 7.3 %collective-permute-start.5 = (f32[256,256]{0,1:T(8,128)S(1)}, f32[256,256]{0,1:T(8,128)S(1)}, u32[]{:S(2)}, u32[]{:S(2)}) collective-permute-start(f32[256,256]{0,1:T(8,128)S(1)} %convolution_bitcast_fusion), channel_id=1, source_target_pairs={{0,4},{4,0},{8,12},{12,8},{1,5},{5,1},{9,13},{13,9},{2,6},{6,2},{1... | collective-permute-start | bytes 786440 | tf_op jit(solution)/shard_map/ppermute | solution.py:10
  120.9 61.5 %copy-start.1 = (bf16[1024,256]{1,0:T(8,128)(2,1)}, bf16[1024,256]{1,0:T(8,128)(2,1)S(1)}, u32[]{:S(2)}) copy-start(bf16[1024,256]{1,0:T(8,128)(2,1)S(1)} %scatter_custom_fusion.3) | copy-start | bytes 1572868
Sparse Core Ops, SparseCore 0:
  18.1 34.6 all-reduce.1
  124.0 58.4 reduce-scatter.3
where the time goes:
time: 190 us; the launch traced here: 189 us
  waiting for transfers between devices  125 us (66%)
  local copies, waits for them, and re-layouts  19 us (10%)
  between operations  15.2 us (8%)
  starting transfers between devices  11.1 us (6%)
  matrix products  9.46 us (5%)
  blocking collectives  7.19 us (4%)
  other arithmetic  2.34 us (1%)
    unnamed x3, waiting for transfers between devices  58.6 us
    ppermute x6, waiting for transfers between devices, partner(): return lax.ppermute(value, axis, pairs)  39.9 us
    psum x1, waiting for transfers between devices, shards(): summed = lax.psum(spread, ('rhs', 'pan'))  26.5 us
    ppermute x6, starting transfers between devices, partner(): return lax.ppermute(value, axis, pairs)  11 us
    all_gather x1, blocking collectives, shards(): loads = lax.all_gather(upper_source, ('rhs', 'pan'), axis=1, tiled=True)  7.19 us
    scatter x1, local copies, waits for them, and re-layouts, shards(): adjoint = jnp.zeros_like(bottom_back).at[order_rows].set(bottom_back)  5.07 us
    gather x1, local copies, waits for them, and re-layouts, shards(): ordered = bottom_source[order_rows] * row_mask  4.57 us
  transfers between devices with their start and end apart: 8, of which 8 were waited for; matrix products, arithmetic and copies ran while one was open for 1% of the time, Pallas kernels for 0%

commit v1 on v0

--- a/solution.py
+++ b/solution.py
@@ -52,7 +52,7 @@
     spread = (
         jnp.zeros((front_size, contrib.shape[1]), jnp.float32).at[bottom_targets[0]].set(contrib)
     )
-    summed = lax.psum(spread, ("rhs", "pan"))
+    summed = jnp.sum(lax.all_gather(spread, ("rhs", "pan")), axis=0)
     loads = lax.all_gather(upper_source, ("rhs", "pan"), axis=1, tiled=True)
     column_count = summed.shape[1]
     front_input = (loads[0:front_size].astype(jnp.float32) - summed).astype(jnp.bfloat16)

time: 190 us -> 181 us (0.953)
  waiting for transfers between devices: 125 us -> 118 us
    psum x1 -> x0, waiting for transfers between devices: 26.5 us -> none  [shards(): summed = lax.psum(spread, ('rhs', 'pan'))]
    all_gather x0 -> x1, waiting for transfers between devices: none -> 12 us  [shards(): summed = jnp.sum(lax.all_gather(spread, ('rhs', 'pan')), axis=0)]
    ppermute x6, waiting for transfers between devices: 39.9 us -> 48.7 us  [partner(): return lax.ppermute(value, axis, pairs)]
  transfers between devices with their start and end apart: 8 -> 8, of which waited for: 8 -> 8; matrix products, arithmetic and copies ran while one was open for 1% -> 0% of each run, Pallas kernels for 0% -> 0%
where the time goes in v1:
time: 181 us
  waiting for transfers between devices  118 us (65%)
  local copies, waits for them, and re-layouts  20 us (11%)
  between operations  15.2 us (8%)
  starting transfers between devices  10.2 us (6%)
  matrix products  7.71 us (4%)
  blocking collectives  7.19 us (4%)
  other arithmetic  3.01 us (2%)
    unnamed x3, waiting for transfers between devices  57 us
    ppermute x6, waiting for transfers between devices, partner(): return lax.ppermute(value, axis, pairs)  48.7 us
    all_gather x1, waiting for transfers between devices, shards(): summed = jnp.sum(lax.all_gather(spread, ('rhs', 'pan')), axis=0)  12 us
    ppermute x6, starting transfers between devices, partner(): return lax.ppermute(value, axis, pairs)  10.1 us
    all_gather x1, blocking collectives, shards(): loads = lax.all_gather(upper_source, ('rhs', 'pan'), axis=1, tiled=True)  7.19 us
    scatter x1, local copies, waits for them, and re-layouts, shards(): adjoint = jnp.zeros_like(bottom_back).at[order_rows].set(bottom_back)  5.07 us
    gather x1, local copies, waits for them, and re-layouts, shards(): ordered = bottom_source[order_rows] * row_mask  4.57 us
  transfers between devices with their start and end apart: 8, of which 8 were waited for; matrix products, arithmetic and copies ran while one was open for 0% of the time, Pallas kernels for 0%

profile of v1, /device:TPU:0, one launch (start us, length us, event | category | flops | bytes accessed | tf_op | source)
XLA Modules:
  0.0 181.1 jit_solution(529740205689723240)
XLA Ops:
  8.0 0.7 compare_select_fusion
  8.7 4.6 %gather_fusion = bf16[1024,256]{1,0:T(8,128)(2,1)S(1)} fusion(bf16[1024,256]{1,0:T(8,128)(2,1)} %param.11, s32[1024]{0:T(1024)S(1)} %broadcast_clamp_fusion), kind=kCustom, calls=%fused_computation | custom fusion | bytes 1052672 | tf_op jit(solution)/shard_map/gather | solution.py:47
  13.4 1.0 fusion.3
  14.4 0.8 copy-done.3
  15.6 0.8 fusion.45
  16.4 1.7 scatter_custom_fusion
  18.2 7.2 %all_gather.9 = bf16[448,256]{0,1:T(8,128)(2,1)S(1)} all-gather(bf16[448,64]{0,1:T(8,128)(2,1)S(1)} %copy-done.7), channel_id=1, replica_groups=mesh['rec'=2,'leaf'=4,'rhs'=2,'pan'=2] {'rhs','pan'}, dimensions={1}, use_global_device_ids=true | all-gather | bytes 286720 | tf_op jit(solution)/shard_map/all_gather | solution.py:56
  25.6 12.0 %all-gather.3.cloned.1.call-done = f32[1024,256]{1,0:T(8,128)} async-done(((f32[256,256]{1,0:T(8,128)}), f32[1024,256]{1,0:T(8,128)}) %all-gather.3.cloned.1.call-update) | async-done | bytes 1048592 | tf_op jit(solution)/shard_map/all_gather | solution.py:55
  37.7 1.3 reduce_sum.9
  39.5 1.1 scatter_custom_fusion.1
  40.7 1.6 collective-permute-start
  42.3 6.8 %collective-permute-done = f32[256,256]{1,0:T(8,128)S(1)} collective-permute-done((f32[256,256]{1,0:T(8,128)S(1)}, f32[256,256]{1,0:T(8,128)S(1)}, u32[]{:S(2)}, u32[]{:S(2)}) %collective-permute-start) | collective-permute-done | bytes 262176 | tf_op jit(solution)/shard_map/ppermute | solution.py:10
  49.7 1.1 scatter_custom_fusion.2
  50.8 1.6 collective-permute-start.1
  52.3 6.1 %collective-permute-done.1 = f32[256,256]{1,0:T(8,128)S(1)} collective-permute-done((f32[256,256]{1,0:T(8,128)S(1)}, f32[256,256]{1,0:T(8,128)S(1)}, u32[]{:S(2)}, u32[]{:S(2)}) %collective-permute-start.1) | collective-permute-done | bytes 262176 | tf_op jit(solution)/shard_map/ppermute | solution.py:10
  58.5 2.5 %collective-permute-start.2 = (f32[256,256]{1,0:T(8,128)S(1)}, f32[256,256]{1,0:T(8,128)S(1)}, u32[]{:S(2)}, u32[]{:S(2)}) collective-permute-start(f32[256,256]{1,0:T(8,128)S(1)} %add.115), channel_id=1, source_target_pairs={{0,8},{4,12},{8,0},{12,4},{1,9},{5,13},{9,1},{13,5},{2,10},{6,14},... | collective-permute-start | bytes 786440 | tf_op jit(solution)/shard_map/ppermute | solution.py:10
  61.0 10.8 %collective-permute-done.2 = f32[256,256]{1,0:T(8,128)S(1)} collective-permute-done((f32[256,256]{1,0:T(8,128)S(1)}, f32[256,256]{1,0:T(8,128)S(1)}, u32[]{:S(2)}, u32[]{:S(2)}) %collective-permute-start.2) | collective-permute-done | bytes 262176 | tf_op jit(solution)/shard_map/ppermute | solution.py:10
  72.2 0.6 collective-permute-start.3
  72.8 6.7 %collective-permute-done.3 = f32[256,256]{0,1:T(8,128)S(1)} collective-permute-done((f32[256,256]{0,1:T(8,128)S(1)}, f32[256,256]{0,1:T(8,128)S(1)}, u32[]{:S(2)}, u32[]{:S(2)}) %collective-permute-start.3) | collective-permute-done | bytes 262176 | tf_op jit(solution)/shard_map/ppermute | solution.py:10
  79.5 3.2 %collective-permute-start.4 = (f32[256,256]{0,1:T(8,128)S(1)}, f32[256,256]{0,1:T(8,128)S(1)}, u32[]{:S(2)}, u32[]{:S(2)}) collective-permute-start(f32[256,256]{0,1:T(8,128)S(1)} %add.117), channel_id=1, source_target_pairs={{0,8},{4,12},{8,0},{12,4},{1,9},{5,13},{9,1},{13,5},{2,10},{6,14},... | collective-permute-start | bytes 786440 | tf_op jit(solution)/shard_map/ppermute | solution.py:10
  82.7 11.6 %collective-permute-done.4 = f32[256,256]{0,1:T(8,128)S(1)} collective-permute-done((f32[256,256]{0,1:T(8,128)S(1)}, f32[256,256]{0,1:T(8,128)S(1)}, u32[]{:S(2)}, u32[]{:S(2)}) %collective-permute-start.4) | collective-permute-done | bytes 262176 | tf_op jit(solution)/shard_map/ppermute | solution.py:10
  94.5 0.8 gather_fusion.1
  95.7 0.7 collective-permute-start.5
  96.4 6.6 %collective-permute-done.5 = f32[256,256]{0,1:T(8,128)S(1)} collective-permute-done((f32[256,256]{0,1:T(8,128)S(1)}, f32[256,256]{0,1:T(8,128)S(1)}, u32[]{:S(2)}, u32[]{:S(2)}) %collective-permute-start.5) | collective-permute-done | bytes 262176 | tf_op jit(solution)/shard_map/ppermute | solution.py:10
  103.2 0.8 gather_fusion.2
  104.5 0.8 gather_fusion.3
  105.4 2.6 %fusion.4 = bf16[1024,256]{0,1:T(8,128)(2,1)} fusion(bf16[1024,1024]{1,0:T(8,128)(2,1)S(1)} %copy-done, bf16[128,256]{1,0:T(8,128)(2,1)S(1)} %gather_fusion.3, bf16[128,1024]{1,0:T(8,128)(2,1)} %param.13, bf16[256,1024]{1,0:T(8,128)(2,1)S(1)} %copy-done.4, f32[1024]{0:T(1024)S(1)} %get-tuple-element.14), kind=kOutput, calls=%fused_computation.15 | convolution fusion | flops 605552640 | bytes 3477504 | tf_op jit(solution)/shard_map/ij,ic->jc/dot_general | solution.py:111
  108.0 1.2 copy.48
  109.3 5.1 %scatter_custom_fusion.3 = bf16[1024,256]{1,0:T(8,128)(2,1)S(1)} fusion(s32[1024]{0:T(1024)S(1)} %bitcast.57, bf16[1024,256]{1,0:T(8,128)(2,1)S(1)} %copy.48, bf16[]{:T(256)} %constant.57.clone.1), kind=kCustom, calls=%fused_computation.42 | custom fusion | bytes 524290 | tf_op jit(solution)/shard_map/scatter | solution.py:114
  114.4 1.9 %fusion.5 = f32[512,256]{0,1:T(8,128)S(1)} fusion(bf16[1024,256]{1,0:T(8,128)(2,1)S(1)} %scatter_custom_fusion.3, bf16[512,1024]{1,0:T(8,128)(2,1)} %param.14), kind=kOutput, calls=%fused_computation.17 | convolution fusion | flops 268566528 | bytes 2097152 | tf_op jit(solution)/shard_map/dot_general | solution.py:116
  116.3 1.0 copy.50
  117.3 56.9 %reduce-scatter.4.cloned.1.call-done = f32[32,256]{1,0:T(8,128)} async-done(((f32[512,256]{1,0:T(8,128)}), f32[32,256]{1,0:T(8,128)}) %reduce-scatter.4.cloned.1.call-update) | async-done | bytes 32784
  (52 shorter events, 3.5 us)
Async XLA Ops:
  7.2 6.2 %copy-start = (bf16[1024,1024]{1,0:T(8,128)(2,1)S(1)}, bf16[1024,1024]{1,0:T(8,128)(2,1)}, u32[]{:S(2)}) copy-start(bf16[1024,1024]{1,0:T(8,128)(2,1)} %param.12) | copy-start | bytes 6291460
  7.2 30.5 %all-gather.3.cloned.1.call-start = ((), (), s32[]{:S(2)}) async-start(), calls=%async_computation.1 | async-start | bytes 1310720 | tf_op jit(solution)/shard_map/all_gather | solution.py:55
  13.3 1.9 %copy-start.6 = (bf16[128,1024]{1,0:T(8,128)(2,1)S(1)}, bf16[128,1024]{1,0:T(8,128)(2,1)}, u32[]{:S(2)}) copy-start(bf16[128,1024]{1,0:T(8,128)(2,1)} %param.13) | copy-start | bytes 786436
  13.3 2.3 %copy-start.8 = (s32[1,128]{1,0:T(1,128)S(1)}, s32[1,128]{1,0:T(1,128)}, u32[]{:S(2)}) copy-start(s32[1,128]{1,0:T(1,128)} %param.17) | copy-start | bytes 1540
  13.4 4.8 %copy-start.7 = (bf16[448,64]{0,1:T(8,128)(2,1)S(1)}, bf16[448,64]{0,1:T(8,128)(2,1)}, u32[]{:S(2)}) copy-start(bf16[448,64]{0,1:T(8,128)(2,1)} %param.18) | copy-start | bytes 172036
  14.4 0.8 copy-start.3
  15.2 23.8 %copy-start.2 = (bf16[448,256]{1,0:T(8,128)(2,1)S(1)}, bf16[448,256]{1,0:T(8,128)(2,1)}, u32[]{:S(2)}) copy-start(bf16[448,256]{1,0:T(8,128)(2,1)} %param.19) | copy-start | bytes 688132
  15.5 23.8 %copy-start.5 = (bf16[128,384]{1,0:T(8,128)(2,1)S(1)}, bf16[128,384]{1,0:T(8,128)(2,1)}, u32[]{:S(2)}) copy-start(bf16[128,384]{1,0:T(8,128)(2,1)} %param.20) | copy-start | bytes 294916
  18.1 156.1 %reduce-scatter.4.cloned.1.call-start = ((), (), s32[]{:S(2)}) async-start(), calls=%async_computation.2 | async-start | bytes 557056
  40.7 8.5 %collective-permute-start = (f32[256,256]{1,0:T(8,128)S(1)}, f32[256,256]{1,0:T(8,128)S(1)}, u32[]{:S(2)}, u32[]{:S(2)}) collective-permute-start(f32[256,256]{1,0:T(8,128)S(1)} %add_dynamic-update-slice_fusion), channel_id=1, source_target_pairs={{0,4},{4,0},{8,12},{12,8},{1,5},{5,1},{9,13},{13,9},{2,6},{6,2},{1... | collective-permute-start | bytes 786440 | tf_op jit(solution)/shard_map/ppermute | solution.py:10
  50.8 7.7 %collective-permute-start.1 = (f32[256,256]{1,0:T(8,128)S(1)}, f32[256,256]{1,0:T(8,128)S(1)}, u32[]{:S(2)}, u32[]{:S(2)}) collective-permute-start(f32[256,256]{1,0:T(8,128)S(1)} %add_dynamic-update-slice_fusion.1), channel_id=1, source_target_pairs={{0,4},{4,0},{8,12},{12,8},{1,5},{5,1},{9,13},{13,9},{2,6},{6,2},{1... | collective-permute-start | bytes 786440 | tf_op jit(solution)/shard_map/ppermute | solution.py:10
  58.5 13.3 %collective-permute-start.2 = (f32[256,256]{1,0:T(8,128)S(1)}, f32[256,256]{1,0:T(8,128)S(1)}, u32[]{:S(2)}, u32[]{:S(2)}) collective-permute-start(f32[256,256]{1,0:T(8,128)S(1)} %add.115), channel_id=1, source_target_pairs={{0,8},{4,12},{8,0},{12,4},{1,9},{5,13},{9,1},{13,5},{2,10},{6,14},... | collective-permute-start | bytes 786440 | tf_op jit(solution)/shard_map/ppermute | solution.py:10
  72.2 7.3 %collective-permute-start.3 = (f32[256,256]{0,1:T(8,128)S(1)}, f32[256,256]{0,1:T(8,128)S(1)}, u32[]{:S(2)}, u32[]{:S(2)}) collective-permute-start(f32[256,256]{0,1:T(8,128)S(1)} %convolution_bitcast_fusion.1), channel_id=1, source_target_pairs={{0,4},{4,0},{8,12},{12,8},{1,5},{5,1},{9,13},{13,9},{2,6},{6,2},{1... | collective-permute-start | bytes 786440 | tf_op jit(solution)/shard_map/ppermute | solution.py:10
  79.5 14.8 %collective-permute-start.4 = (f32[256,256]{0,1:T(8,128)S(1)}, f32[256,256]{0,1:T(8,128)S(1)}, u32[]{:S(2)}, u32[]{:S(2)}) collective-permute-start(f32[256,256]{0,1:T(8,128)S(1)} %add.117), channel_id=1, source_target_pairs={{0,8},{4,12},{8,0},{12,4},{1,9},{5,13},{9,1},{13,5},{2,10},{6,14},... | collective-permute-start | bytes 786440 | tf_op jit(solution)/shard_map/ppermute | solution.py:10
  94.3 11.0 %copy-start.4 = (bf16[256,1024]{1,0:T(8,128)(2,1)S(1)}, bf16[256,1024]{1,0:T(8,128)(2,1)}, u32[]{:S(2)}) copy-start(bf16[256,1024]{1,0:T(8,128)(2,1)} %copy-done.3) | copy-start | bytes 1572868
  95.7 7.4 %collective-permute-start.5 = (f32[256,256]{0,1:T(8,128)S(1)}, f32[256,256]{0,1:T(8,128)S(1)}, u32[]{:S(2)}, u32[]{:S(2)}) collective-permute-start(f32[256,256]{0,1:T(8,128)S(1)} %convolution_bitcast_fusion), channel_id=1, source_target_pairs={{0,4},{4,0},{8,12},{12,8},{1,5},{5,1},{9,13},{13,9},{2,6},{6,2},{1... | collective-permute-start | bytes 786440 | tf_op jit(solution)/shard_map/ppermute | solution.py:10
  114.3 59.9 %copy-start.1 = (bf16[1024,256]{1,0:T(8,128)(2,1)}, bf16[1024,256]{1,0:T(8,128)(2,1)S(1)}, u32[]{:S(2)}) copy-start(bf16[1024,256]{1,0:T(8,128)(2,1)S(1)} %scatter_custom_fusion.3) | copy-start | bytes 1572868
Sparse Core Ops, SparseCore 0:
  18.2 19.4 all-gather.2
  117.4 56.7 reduce-scatter.3
